TPU v7x, 32 devices: a whole 2x2x4 slice. The times are simulated.
32 devices in a mesh: rows: 8 (over z, x), cols: 4 (over y, core).
Axes of the slice: x: 2, y: 2, z: 4, core: 2. Of those that a mesh axis runs over, the one named last changes fastest.
Arguments:
- hankel: float32 [256, 32768], P('rows', 'cols'), may hold values from -6 to 6
- shifted: float32 [256, 32768], P('rows', 'cols'), may hold values from -6 to 6
- start_basis: float32 [32768, 128], P(('cols', 'rows')), may hold values from -0.03125 to 0.03125
Outputs:
- basis: float32 [256, 128], P('rows')
- operator: float32 [128, 128], replicated
All inputs are finite; a program needn't handle non-finite values.
Results may differ from a plain program's by a relative error of at most 0.0002.
Values sent between devices are 32-bit elements; how exact they have to be, the bound alone decides.
A program may use at most 64 MiB of HBM per device.

v0:
```python
import math

import jax
import jax.numpy as jnp
from jax import lax
from jax.sharding import PartitionSpec as P


def product(left, right):
    return jnp.dot(left, right, precision=lax.Precision.HIGHEST, preferred_element_type=jnp.float32)


def right_solve(values, lower):
    return lax.linalg.triangular_solve(lower, values, left_side=False, lower=True, transpose_a=True)


def reduce_columns(y_part, slab, col_index):
    y_full = lax.psum(y_part, "cols")
    return (y_full, lax.dynamic_slice_in_dim(y_full, col_index * slab, slab, 0))


def factor(y_slice, total):
    gram = lax.psum(product(y_slice.T, y_slice) / total, ("rows", "cols"))
    return jnp.linalg.cholesky(gram)


def left_rows(y_full, lower, slab, col_index):
    u_full = right_solve(y_full, lower)
    return (u_full, lax.dynamic_slice_in_dim(u_full, col_index * slab, slab, 0))


def on_device(hankel, shifted, start_basis):
    rows_dev, cols_dev = hankel.shape
    total = rows_dev * lax.axis_size("rows")
    slab = rows_dev // lax.axis_size("cols")
    col_index = lax.axis_index("cols")
    inv_root = 1.0 / math.sqrt(total)
    block = hankel
    y_part = product(block, lax.all_gather(start_basis, "rows", axis=0, tiled=True))
    y_full, y_slice = reduce_columns(y_part, slab, col_index)
    lower = factor(y_slice, total)
    u_full, u_slice = left_rows(y_full, lower, slab, col_index)
    block = hankel
    w_slice = lax.psum_scatter(product(block.T, u_full), "rows", scatter_dimension=0, tiled=True)
    lower_w = jnp.linalg.cholesky(lax.psum(product(w_slice.T, w_slice), ("rows", "cols")))
    operand = right_solve(w_slice, lower_w)
    piece = lax.all_gather(operand, "rows", axis=0, tiled=True)
    block = hankel
    y_part = product(block, piece)
    z_part = product(shifted, piece)
    y_full, z_full = lax.psum((y_part, z_part), "cols")
    y_slice = lax.dynamic_slice_in_dim(y_full, col_index * slab, slab, 0)
    z_slice = lax.dynamic_slice_in_dim(z_full, col_index * slab, slab, 0)
    gram, cross = lax.psum(
        (product(y_slice.T, y_slice) / total, product(y_slice.T, z_slice) * inv_root),
        ("rows", "cols"),
    )
    lower = jnp.linalg.cholesky(gram)
    u_full, u_slice = left_rows(y_full, lower, slab, col_index)
    operator = lax.linalg.triangular_solve(lower, cross, left_side=True, lower=True)
    return (u_full, operator)


def solution(mesh):
    return jax.shard_map(
        on_device,
        mesh=mesh,
        in_specs=(P("rows", "cols"), P("rows", "cols"), P(("cols", "rows"), None)),
        out_specs=(P("rows", None), P()),
        check_vma=False,
    )
```

profile of v0, /device:TPU:0, one launch (start us, length us, event | category | flops | bytes accessed | tf_op | source)
XLA Modules:
  0.0 742.9 jit_solution(10276179012910582466)
XLA Ops:
  8.0 78.3 %all-gather.3.cloned.1.call-done = f32[8192,128]{1,0:T(8,128)} async-done(((f32[1024,128]{1,0:T(8,128)}), f32[8192,128]{1,0:T(8,128)}) %all-gather.3.cloned.1.call-update) | async-done | bytes 4194320 | tf_op jit(solution)/shard_map/all_gather | solution.py:39
  86.3 4.0 fusion.23
  90.3 10.1 %psum.49 = f32[32,128]{1,0:T(8,128)S(1)} all-reduce(f32[32,128]{1,0:T(8,128)S(1)} %fusion.23), channel_id=1, replica_groups=mesh['rows'=8,'cols'=4] {'cols'}, use_global_device_ids=true, to_apply=%region_0.0 | all-reduce | flops 4096 | bytes 32768 | tf_op jit(solution)/shard_map/psum | solution.py:18
  101.4 116.0 %all-reduce.6.cloned.1.call-done = f32[128,128]{0,1:T(8,128)} async-done(((f32[128,128]{0,1:T(8,128)}), f32[128,128]{0,1:T(8,128)}) %all-reduce.6.cloned.1.call-update) | async-done | bytes 65552 | tf_op jit(solution)/shard_map/psum | solution.py:23
  219.2 11.7 %cholesky.59 = f32[128,128]{1,0:T(8,128)S(1)} custom-call(f32[128,128]{1,0:T(8,128)S(1)} %fusion.11), custom_call_target="Cholesky" | custom-call | tf_op jit(solution)/shard_map/jit(cholesky)/cholesky | solution.py:24
  232.3 9.8 %custom-call.14 = f32[1,128,128]{1,2,0:T(8,128)S(1)} custom-call(f32[1,128,128]{2,1,0:T(8,128)S(1)} %fusion), custom_call_target="InvertDiagBlocksLowerTriangular" | custom-call | tf_op jit(solution)/shard_map/triangular_solve/custom-call.0 | solution.py:14
  242.4 4.9 convolution_bitcast_fusion
  247.4 89.3 %reduce-scatter.2.cloned.1.call-done = f32[1024,128]{0,1:T(8,128)} async-done(((f32[8192,128]{0,1:T(8,128)}), f32[1024,128]{0,1:T(8,128)}) %reduce-scatter.2.cloned.1.call-update) | async-done | bytes 524304 | tf_op jit(solution)/shard_map/reduce_scatter | solution.py:44
  336.7 2.4 fusion.24
  339.4 121.6 %all-reduce.8.cloned.1.call-done = f32[128,128]{0,1:T(8,128)} async-done(((f32[128,128]{0,1:T(8,128)}), f32[128,128]{0,1:T(8,128)}) %all-reduce.8.cloned.1.call-update) | async-done | bytes 65552 | tf_op jit(solution)/shard_map/psum | solution.py:45
  461.0 0.9 copy.8
  462.8 11.7 %cholesky.70 = f32[128,128]{1,0:T(8,128)S(1)} custom-call(f32[128,128]{1,0:T(8,128)S(1)} %fusion.9), custom_call_target="Cholesky" | custom-call | tf_op jit(solution)/shard_map/jit(cholesky)/cholesky | solution.py:45
  475.9 9.8 %custom-call.11 = f32[1,128,128]{1,2,0:T(8,128)S(1)} custom-call(f32[1,128,128]{2,1,0:T(8,128)S(1)} %fusion.1), custom_call_target="InvertDiagBlocksLowerTriangular" | custom-call | tf_op jit(solution)/shard_map/triangular_solve | solution.py:14
  485.7 2.9 fusion.7
  488.8 74.1 %all-gather.5.cloned.1.call-done = f32[8192,128]{1,0:T(8,128)} async-done(((f32[1024,128]{1,0:T(8,128)}), f32[8192,128]{1,0:T(8,128)}) %all-gather.5.cloned.1.call-update) | async-done | bytes 4194320 | tf_op jit(solution)/shard_map/all_gather | solution.py:47
  562.9 4.4 convolution_bitcast_fusion.4
  567.4 6.7 convolution_bitcast_fusion.1
  574.1 11.2 %all-reduce.1 = (f32[32,128]{1,0:T(8,128)S(1)}, f32[32,128]{0,1:T(8,128)S(1)}) all-reduce(f32[32,128]{1,0:T(8,128)S(1)} %convolution_bitcast_fusion.4, f32[32,128]{0,1:T(8,128)S(1)} %convolution_bitcast_fusion.1), channel_id=1, replica_groups=mesh['rows'=8,'cols'=4] {'cols'}, use_global_device_ids=true, to_apply=%region_6.9 | all-reduce | flops 8192 | bytes 65536 | tf_op jit(solution)/shard_map/psum | solution.py:51
  585.3 0.9 convolution_multiply_fusion.1
  586.2 0.9 convolution_multiply_fusion
  587.2 121.6 %all-reduce.10.cloned.1.call-done = (f32[128,128]{0,1:T(8,128)}, f32[128,128]{1,0:T(8,128)}) async-done(((f32[128,128]{0,1:T(8,128)}, f32[128,128]{1,0:T(8,128)}), (f32[128,128]{0,1:T(8,128)}, f32[128,128]{1,0:T(8,128)})) %all-reduce.10.cloned.1.call-update) | async-done | bytes 131088 | tf_op jit(solution)/shard_map/psum | solution.py:54
  710.6 11.7 %cholesky.81 = f32[128,128]{1,0:T(8,128)S(1)} custom-call(f32[128,128]{1,0:T(8,128)S(1)} %fusion.6), custom_call_target="Cholesky" | custom-call | tf_op jit(solution)/shard_map/jit(cholesky)/cholesky | solution.py:58
  723.7 9.8 %custom-call.15 = f32[1,128,128]{1,2,0:T(8,128)S(1)} custom-call(f32[1,128,128]{2,1,0:T(8,128)S(1)} %fusion.2), custom_call_target="InvertDiagBlocksLowerTriangular" | custom-call | tf_op jit(solution)/shard_map/triangular_solve/custom-call.0 | solution.py:14
  734.3 1.8 fusion.3
  (35 shorter events, 11.8 us)
Async XLA Ops:
  7.2 79.1 %copy-start = (f32[32,8192]{1,0:T(8,128)S(1)}, f32[32,8192]{1,0:T(8,128)}, u32[]{:S(2)}) copy-start(f32[32,8192]{1,0:T(8,128)} %param.6) | copy-start | bytes 3145732
  7.2 79.1 %all-gather.3.cloned.1.call-start = ((), (), s32[]{:S(2)}) async-start(), calls=%async_computation.1 | async-start | bytes 4718592 | tf_op jit(solution)/shard_map/all_gather | solution.py:39
  7.9 209.5 %all-reduce.6.cloned.1.call-start = ((), (), s32[]{:S(2)}) async-start(), calls=%async_computation.2 | async-start | bytes 131072 | tf_op jit(solution)/shard_map/psum | solution.py:23
  101.4 235.3 %reduce-scatter.2.cloned.1.call-start = ((), (), s32[]{:S(2)}) async-start(), calls=%async_computation.3 | async-start | bytes 4718592 | tf_op jit(solution)/shard_map/reduce_scatter | solution.py:44
  247.3 320.0 %copy-start.2 = (f32[32,8192]{1,0:T(8,128)S(1)}, f32[32,8192]{1,0:T(8,128)}, u32[]{:S(2)}) copy-start(f32[32,8192]{1,0:T(8,128)} %param.7) | copy-start | bytes 3145732
  247.3 213.7 %all-reduce.8.cloned.1.call-start = ((), (), s32[]{:S(2)}) async-start(), calls=%async_computation.4 | async-start | bytes 131072 | tf_op jit(solution)/shard_map/psum | solution.py:45
  339.2 223.7 %all-gather.5.cloned.1.call-start = ((), (), s32[]{:S(2)}) async-start(), calls=%async_computation.5 | async-start | bytes 4718592 | tf_op jit(solution)/shard_map/all_gather | solution.py:47
  488.5 220.3 %all-reduce.10.cloned.1.call-start = ((), (), s32[]{:S(2)}) async-start(), calls=%async_computation.6 | async-start | bytes 262144 | tf_op jit(solution)/shard_map/psum | solution.py:54
  562.9 4.5 copy-start.1
Sparse Core Ops, SparseCore 0:
  10.1 76.0 all-gather.2
  101.5 115.8 all-reduce.5
  247.4 89.2 reduce-scatter.1
  343.7 117.3 all-reduce.7
  488.7 74.1 all-gather.4
  587.3 121.4 all-reduce.9
where the time goes:
time: 743 us
  waiting for transfers between devices  602 us (81%)
  other arithmetic  71.1 us (10%)
  matrix products  30.9 us (4%)
  blocking collectives  21.3 us (3%)
  between operations  14.3 us (2%)
    psum x1, waiting for transfers between devices, on_device(): lax.psum((product(y_slice.T, y_slice) / total, product(y_slice.T, z_slice...  122 us
    psum x1, waiting for transfers between devices, on_device(): lax.psum(product(w_slice.T, w_slice), ('rows', 'cols'))  122 us
    psum x1, waiting for transfers between devices, factor(): gram = lax.psum(product(y_slice.T, y_slice) / total, ('rows', 'cols'))  116 us
    reduce_scatter x1, waiting for transfers between devices, on_device(): lax.psum_scatter(product(block.T, u_full), 'rows', scatter_dimension=0, t...  89.3 us
    all_gather x1, waiting for transfers between devices, on_device(): lax.all_gather(start_basis, 'rows', axis=0, tiled=True)  78.3 us
    all_gather x1, waiting for transfers between devices, on_device(): piece = lax.all_gather(operand, 'rows', axis=0, tiled=True)  74.1 us
    another operation x6, other arithmetic, right_solve(): lax.linalg.triangular_solve(lower, values, left_side=False, lower=True, t...  31.4 us
    dot_general x8, matrix products, product(): jnp.dot(left, right, precision=lax.Precision.HIGHEST, preferred_element_t...  25.3 us
  transfers between devices with their start and end apart: 6, of which 6 were waited for; matrix products, arithmetic and copies ran while one was open for 0% of the time, Pallas kernels for 0%

commit v1 on v0

v1 whole, which is shorter than its diff:
```python
import functools
import math

import jax
import jax.numpy as jnp
from jax import lax
from jax.experimental import pallas as pl
from jax.experimental.pallas import tpu as pltpu
from jax.sharding import PartitionSpec as P

MESH = pl.DeviceIdType.MESH
NT = (((1,), (1,)), ((), ()))
VMEM_LIMIT = 48 * 1024 * 1024


def product(left, right, dims=(((1,), (0,)), ((), ()))):
    return lax.dot_general(
        left, right, dims, precision=lax.Precision.HIGHEST, preferred_element_type=jnp.float32
    )


def wait_bytes(ref, sem):
    pltpu.make_async_copy(ref, ref, sem).wait()


def exchange_kernel(
    n_rows, n_cols, hankel, shifted, start, y_out, c_out, z_out,
    h_slab, s_slab, parts, landed, sums, local_sem, slab_send, slab_recv, part_send, part_recv, sum_send, sum_recv,
):
    n = n_rows * n_cols
    row, col = lax.axis_index("rows"), lax.axis_index("cols")
    me = col * n_rows + row
    sub = h_slab.shape[2]
    prefixes = y_out.shape[0]
    share = prefixes // n

    def others(body):
        def step(k, carry):
            other = lax.rem(me + k, n)
            body(k, {"rows": lax.rem(other, n_rows), "cols": other // n_rows})
            return carry

        lax.fori_loop(1, n, step, 0)

    def own_copy(source, slab, which):
        columns = pl.ds(pl.multiple_of(row * sub, sub), sub)
        return pltpu.make_async_copy(source.at[:, columns], slab.at[row], local_sem.at[which])

    def send_slabs(source, slab, which):
        def step(k, carry):
            there = lax.rem(row + k, n_rows)
            columns = pl.ds(pl.multiple_of(there * sub, sub), sub)
            pltpu.make_async_remote_copy(
                src_ref=source.at[:, columns],
                dst_ref=slab.at[row],
                send_sem=slab_send.at[which],
                recv_sem=slab_recv.at[which],
                device_id={"rows": there, "cols": col},
                device_id_type=MESH,
            ).start()
            return carry

        lax.fori_loop(1, n_rows, step, 0)

    def whole(slab):
        return slab[...].reshape(prefixes, sub)

    def scatter(value, which):
        if share % 8 == 0:
            parts[which] = value.reshape(n, share, value.shape[1])
        else:
            for i in range(n):
                parts[which, i] = value[i * share : (i + 1) * share]
        landed[which, 0] = parts[which, me]

        def body(k, device):
            other = lax.rem(me + k, n)
            pltpu.make_async_remote_copy(
                src_ref=parts.at[which, other],
                dst_ref=landed.at[which, k],
                send_sem=part_send.at[which],
                recv_sem=part_recv.at[which],
                device_id=device,
                device_id_type=MESH,
            ).start()

        others(body)

    def gather(which):
        wait_bytes(landed.at[which, pl.ds(1, n - 1)], part_recv.at[which])
        sums[which, me] = jnp.sum(landed[which], axis=0)

        def body(k, device):
            pltpu.make_async_remote_copy(
                src_ref=sums.at[which, me],
                dst_ref=sums.at[which, me],
                send_sem=sum_send.at[which],
                recv_sem=sum_recv.at[which],
                device_id=device,
                device_id_type=MESH,
            ).start()

        others(body)

    def gathered(which, out):
        wait_bytes(sums.at[which, pl.ds(0, n - 1)], sum_recv.at[which])
        if share % 8 == 0:
            out[...] = sums[which].reshape(out.shape)
        else:
            for i in range(n):
                out[i * share : (i + 1) * share, :] = sums[which, i]

    own_copy(hankel, h_slab, 0).start()
    own_copy(shifted, s_slab, 1).start()
    barrier = pltpu.get_barrier_semaphore()
    others(lambda k, device: pl.semaphore_signal(barrier, inc=1, device_id=device, device_id_type=MESH))
    pl.semaphore_wait(barrier, n - 1)

    send_slabs(hankel, h_slab, 0)
    own_copy(hankel, h_slab, 0).wait()
    wait_bytes(h_slab.at[pl.ds(0, n_rows - 1)], slab_recv.at[0])
    scatter(product(whole(h_slab), start[...]), 0)
    send_slabs(shifted, s_slab, 1)
    block = whole(h_slab)
    gram = product(block, block, NT)
    gather(0)
    gathered(0, y_out)
    scatter(product(gram, y_out[...]), 1)
    gather(1)
    gathered(1, c_out)

    own_copy(shifted, s_slab, 1).wait()
    wait_bytes(s_slab.at[pl.ds(0, n_rows - 1)], slab_recv.at[1])
    cross = product(whole(s_slab), whole(h_slab), NT)
    scatter(product(cross, y_out[...]), 2)
    gather(2)
    gathered(2, z_out)

    for which in range(2):
        wait_bytes(h_slab.at[pl.ds(0, n_rows - 1)], slab_send.at[which])
    for which in range(3):
        wait_bytes(parts.at[which, pl.ds(0, n - 1)], part_send.at[which])
        wait_bytes(sums.at[which, pl.ds(0, n - 1)], sum_send.at[which])


def exchange(hankel, shifted, start):
    n_rows, n_cols = lax.axis_size("rows"), lax.axis_size("cols")
    n = n_rows * n_cols
    rows_dev, cols_dev = hankel.shape
    prefixes, sub, rank = rows_dev * n_rows, cols_dev // n_rows, start.shape[1]
    result = jax.ShapeDtypeStruct((prefixes, rank), jnp.float32)
    return pl.pallas_call(
        functools.partial(exchange_kernel, n_rows, n_cols),
        out_shape=[result] * 3,
        in_specs=[pl.BlockSpec(memory_space=pl.ANY)] * 2 + [pl.BlockSpec(memory_space=pltpu.VMEM)],
        out_specs=[pl.BlockSpec(memory_space=pltpu.VMEM)] * 3,
        scratch_shapes=[
            pltpu.VMEM((n_rows, rows_dev, sub), jnp.float32),
            pltpu.VMEM((n_rows, rows_dev, sub), jnp.float32),
            pltpu.VMEM((3, n, prefixes // n, rank), jnp.float32),
            pltpu.VMEM((3, n, prefixes // n, rank), jnp.float32),
            pltpu.VMEM((3, n, prefixes // n, rank), jnp.float32),
            pltpu.SemaphoreType.DMA((2,)),
            pltpu.SemaphoreType.DMA((2,)),
            pltpu.SemaphoreType.DMA((2,)),
            pltpu.SemaphoreType.DMA((3,)),
            pltpu.SemaphoreType.DMA((3,)),
            pltpu.SemaphoreType.DMA((3,)),
            pltpu.SemaphoreType.DMA((3,)),
        ],
        compiler_params=pltpu.CompilerParams(
            collective_id=0, has_side_effects=True, vmem_limit_bytes=VMEM_LIMIT
        ),
    )(hankel, shifted, start)


def invert_factors(grams, outs):
    size = grams[0].shape[0]
    lane = lax.broadcasted_iota(jnp.int32, (8, size), 1)
    sublane = lax.broadcasted_iota(jnp.int32, (8, size), 0)
    line = lax.broadcasted_iota(jnp.int32, (1, size), 1)
    tiles = [[gram[i : i + 8] for i in range(0, size, 8)] for gram in grams]
    for j in range(size):
        first, r = divmod(j, 8)
        for held, out in zip(tiles, outs):
            pivot = held[first][r : r + 1]
            diagonal = pivot[:, j : j + 1]
            inverse = 1.0 / diagonal
            scaled = jnp.broadcast_to(jnp.where(line == j, inverse, pivot * inverse), (8, size))
            out[j : j + 1, :] = jnp.where(line < j, pivot, jnp.where(line == j, 1.0, 0.0)) * lax.rsqrt(diagonal)
            for i in range(first, size // 8):
                column = held[i][:, j : j + 1]
                kept = jnp.where(lane == j, 0.0, held[i]) - column * scaled
                held[i] = jnp.where(sublane > r, kept, held[i]) if i == first else kept


def factor_kernel(y_ref, c_ref, z_ref, basis_ref, operator_ref, right_inv, left_inv):
    prefixes = c_ref.shape[0]
    rows_dev = basis_ref.shape[0]
    c = c_ref[...]
    c_t = c.T
    right_gram = product(y_ref[...].T, c)
    left_gram = product(c_t, c) * (1.0 / prefixes)
    crossed = product(c_t, z_ref[...]) * (1.0 / math.sqrt(prefixes))
    invert_factors((right_gram, left_gram), (right_inv, left_inv))
    mine = pl.ds(pl.multiple_of(lax.axis_index("rows") * rows_dev, rows_dev), rows_dev)
    basis_ref[...] = product(c_ref[mine, :], left_inv[...], NT)
    operator_ref[...] = product(product(left_inv[...], crossed), right_inv[...], NT)


def on_device(hankel, shifted, start_basis):
    y, c, z = exchange(hankel, shifted, start_basis)
    rank = start_basis.shape[1]
    return pl.pallas_call(
        factor_kernel,
        out_shape=[
            jax.ShapeDtypeStruct((hankel.shape[0], rank), jnp.float32),
            jax.ShapeDtypeStruct((rank, rank), jnp.float32),
        ],
        in_specs=[pl.BlockSpec(memory_space=pltpu.VMEM)] * 3,
        out_specs=[pl.BlockSpec(memory_space=pltpu.VMEM)] * 2,
        scratch_shapes=[pltpu.VMEM((rank, rank), jnp.float32)] * 2,
        compiler_params=pltpu.CompilerParams(vmem_limit_bytes=VMEM_LIMIT),
    )(y, c, z)


def solution(mesh):
    return jax.shard_map(
        on_device,
        mesh=mesh,
        in_specs=(P("rows", "cols"), P("rows", "cols"), P(("cols", "rows"), None)),
        out_specs=(P("rows", None), P()),
        check_vma=False,
    )
```

time: 743 us -> 104 us (0.14)
  waiting for transfers between devices: 602 us -> 0 us
  Pallas kernels: 0 us -> 100 us
  other arithmetic: 71.1 us -> 0 us
  matrix products: 30.9 us -> 0 us
  blocking collectives: 21.3 us -> 0 us
  between operations: 14.3 us -> 0.65 us
    psum x3 -> x0, waiting for transfers between devices: 359 us -> none  [the longest x1 122 us: on_device(): lax.psum((product(y_slice.T, y_slice) / total, product(y_slice.T, z_slice...]
    all_gather x2 -> x0, waiting for transfers between devices: 152 us -> none  [the longest x1 78.3 us: on_device(): lax.all_gather(start_basis, 'rows', axis=0, tiled=True)]
    pallas_call x0 -> x2, Pallas kernels: none -> 100 us  [the longest x1 86.9 us: exchange(): pl.pallas_call(functools.partial(exchange_kernel, n_rows, n_cols), out_sh...]
    reduce_scatter x1 -> x0, waiting for transfers between devices: 89.3 us -> none  [on_device(): lax.psum_scatter(product(block.T, u_full), 'rows', scatter_dimension=0, t...]
    another operation x15 -> x0, other arithmetic: 68.6 us -> none  [the longest x6 31.4 us: right_solve(): lax.linalg.triangular_solve(lower, values, left_side=False, lower=True, t...]
    dot_general x8 -> x0, matrix products: 25.3 us -> none  [product(): jnp.dot(left, right, precision=lax.Precision.HIGHEST, preferred_element_t...]
    psum x2 -> x0, blocking collectives: 21.3 us -> none  [the longest x1 11.2 us: on_device(): y_full, z_full = lax.psum((y_part, z_part), 'cols')]
  transfers between devices with their start and end apart: 6 -> 0, of which waited for: 6 -> 0; matrix products, arithmetic and copies ran while one was open for 0% -> 0% of each run, Pallas kernels for 0% -> 0%
where the time goes in v1:
time: 104 us
  Pallas kernels  100 us (96%)
  local copies, waits for them, and re-layouts  3.48 us (3%)
    pallas_call x1, Pallas kernels, exchange(): pl.pallas_call(functools.partial(exchange_kernel, n_rows, n_cols), out_sh...  86.9 us
    pallas_call x1, Pallas kernels, on_device(): pl.pallas_call(factor_kernel, out_shape=[jax.ShapeDtypeStruct((hankel.sha...  13.1 us
    unnamed x6, local copies, waits for them, and re-layouts  3.48 us

profile of v1, /device:TPU:0, one launch (start us, length us, event | category | flops | bytes accessed | tf_op | source)
XLA Modules:
  0.0 104.2 jit_solution(3533832101746356736)
XLA Ops:
  0.6 0.0 copy-start
  0.6 1.2 %copy-done = f32[32,8192]{1,0:T(8,128)S(1)} copy-done((f32[32,8192]{1,0:T(8,128)S(1)}, f32[32,8192]{1,0:T(8,128)}, u32[]{:S(2)}) %copy-start) | copy-done | bytes 1048600
  1.9 0.0 copy-start.1
  1.9 1.2 %copy-done.1 = f32[32,8192]{1,0:T(8,128)S(1)} copy-done((f32[32,8192]{1,0:T(8,128)S(1)}, f32[32,8192]{1,0:T(8,128)}, u32[]{:S(2)}) %copy-start.1) | copy-done | bytes 1048600
  3.1 0.0 copy-start.2
  3.1 1.0 copy-done.2
  4.1 86.9 %shard_map.50 = (f32[256,128]{1,0:T(8,128)S(1)}, f32[256,128]{1,0:T(8,128)S(1)}, f32[256,128]{1,0:T(8,128)S(1)}) custom-call(f32[32,8192]{1,0:T(8,128)S(1)} %copy-done, f32[32,8192]{1,0:T(8,128)S(1)} %copy-done.1, f32[1024,128]{1,0:T(8,128)S(1)} %copy-done.2), custom_call_target="tpu_custom_call" | custom-call | tf_op jit(solution)/shard_map/pallas_call | solution.py:152
  91.1 13.1 %shard_map.51 = (f32[32,128]{1,0:T(8,128)}, f32[128,128]{1,0:T(8,128)}) custom-call(f32[256,128]{1,0:T(8,128)S(1)} %get-tuple-element.5.y_ref, f32[256,128]{1,0:T(8,128)S(1)} %get-tuple-element.6.c_ref, f32[256,128]{1,0:T(8,128)S(1)} %get-tuple-element.7.z_ref), custom_call_target="tpu_custom_call" | custom-call | tf_op jit(solution)/shard_map/pallas_call | solution.py:214
Async XLA Ops:
  0.6 1.2 %copy-start = (f32[32,8192]{1,0:T(8,128)S(1)}, f32[32,8192]{1,0:T(8,128)}, u32[]{:S(2)}) copy-start(f32[32,8192]{1,0:T(8,128)} %hankel.1) | copy-start | bytes 3145732
  1.9 1.2 %copy-start.1 = (f32[32,8192]{1,0:T(8,128)S(1)}, f32[32,8192]{1,0:T(8,128)}, u32[]{:S(2)}) copy-start(f32[32,8192]{1,0:T(8,128)} %shifted.1) | copy-start | bytes 3145732
  3.1 1.0 copy-start.2

commit v2 on v0

v2 whole, which is shorter than its diff:
```python
import functools
import math

import jax
import jax.numpy as jnp
from jax import lax
from jax.experimental import pallas as pl
from jax.experimental.pallas import tpu as pltpu
from jax.sharding import PartitionSpec as P

MESH = pl.DeviceIdType.MESH
NT = (((1,), (1,)), ((), ()))
VMEM_LIMIT = 48 * 1024 * 1024


def product(left, right, dims=(((1,), (0,)), ((), ()))):
    return lax.dot_general(
        left, right, dims, precision=lax.Precision.HIGHEST, preferred_element_type=jnp.float32
    )


def wait_bytes(ref, sem):
    pltpu.make_async_copy(ref, ref, sem).wait()


def eliminate(begin, end, grams):
    size = grams[0].shape[0]
    height = 8
    lane = lax.broadcasted_iota(jnp.int32, (size, size), 1)
    place = lax.broadcasted_iota(jnp.int32, (size, size), 0)
    line = lax.broadcasted_iota(jnp.int32, (1, size), 1)

    def block(b, held):
        held = list(held)
        pending = size - height * b
        for r in range(height):
            active = (place > r) & (place < pending)
            known = (line < r) | (line >= pending)
            for m, values in enumerate(held):
                pivot = values[r : r + 1]
                diagonal = pivot[:, r : r + 1]
                inverse = 1.0 / diagonal
                scaled = jnp.where(line == r, inverse, pivot * inverse)
                final = jnp.where(known, pivot, jnp.where(line == r, 1.0, 0.0)) * lax.rsqrt(diagonal)
                kept = jnp.where(lane == r, 0.0, values) - values[:, r : r + 1] * scaled
                held[m] = jnp.where(active, kept, jnp.where(place == r, final, values))
        return tuple(
            pltpu.roll(jnp.concatenate([values[height:], values[:height]], axis=0), size - height, 1)
            for values in held
        )

    return lax.fori_loop(begin, end, block, grams)


def spectral_kernel(
    n_rows, n_cols, near, hankel, shifted, start, basis_out, operator_out,
    h_slab, s_slab, begun, parts, landed, middle, sums, local_sem, slab_send, slab_recv,
    part_send, part_recv, mid_send, mid_recv, sum_send, sum_recv,
):
    row, col = lax.axis_index("rows"), lax.axis_index("cols")
    layer, place = row // near, lax.rem(row, near)
    n_layers, n_group = n_rows // near, near * n_cols
    me = col * near + place
    rows_dev, sub = h_slab.shape[1:]
    prefixes = rows_dev * n_rows
    share = prefixes // n_group
    pieces = rows_dev // 8

    def loop(count, body):
        def step(k, carry):
            body(k)
            return carry

        lax.fori_loop(1, count, step, 0)

    def in_group(k):
        other = lax.rem(me + k, n_group)
        return other, {"rows": layer * near + lax.rem(other, near), "cols": other // near}

    def in_rows(k):
        other = lax.rem(row + k, n_rows)
        return other, {"rows": other, "cols": col}

    def in_layers(k):
        other = lax.rem(layer + k, n_layers)
        return other, {"rows": other * near + place, "cols": col}

    def send(source, target, sent, received, device):
        pltpu.make_async_remote_copy(
            src_ref=source,
            dst_ref=target,
            send_sem=sent,
            recv_sem=received,
            device_id=device,
            device_id_type=MESH,
        ).start()

    def own_columns(index):
        return pl.ds(pl.multiple_of(index * sub, sub), sub)

    def own_copy(source, slab, which):
        return pltpu.make_async_copy(source.at[:, own_columns(row)], slab.at[row], local_sem.at[which])

    def send_slabs(source, slab, which, lines):
        def body(k):
            other, device = in_rows(k)
            send(
                source.at[lines, own_columns(other)],
                slab.at[row, lines],
                slab_send.at[which],
                slab_recv.at[which],
                device,
            )

        loop(n_rows, body)

    def send_piece(piece):
        send_slabs(shifted, s_slab, 1, pl.ds(8 * piece, 8))

    def whole(slab):
        return slab[...].reshape(prefixes, sub)

    def scatter(value, which):
        parts[which] = value.reshape(n_group, share, value.shape[1])
        landed[which, 0] = parts[which, me]

        def body(k):
            other, device = in_group(k)
            send(parts.at[which, other], landed.at[which, k], part_send.at[which], part_recv.at[which], device)

        loop(n_group, body)

    def across(which):
        wait_bytes(landed.at[which, pl.ds(1, n_group - 1)], part_recv.at[which])
        middle[which, layer] = jnp.sum(landed[which], axis=0)
        mine = middle.at[which, layer]
        loop(n_layers, lambda k: send(mine, mine, mid_send.at[which], mid_recv.at[which], in_layers(k)[1]))

    def spread(which):
        wait_bytes(middle.at[which, pl.ds(0, n_layers - 1)], mid_recv.at[which])
        sums[which, me] = jnp.sum(middle[which], axis=0)
        mine = sums.at[which, me]
        loop(n_group, lambda k: send(mine, mine, sum_send.at[which], sum_recv.at[which], in_group(k)[1]))

    def total(which):
        wait_bytes(sums.at[which, pl.ds(0, n_group - 1)], sum_recv.at[which])
        return sums[which].reshape(prefixes, sums.shape[3])

    own_copy(hankel, h_slab, 0).start()
    own_copy(shifted, s_slab, 1).start()
    begin_copy = pltpu.make_async_copy(start, begun, local_sem.at[2])
    begin_copy.start()
    barrier = pltpu.get_barrier_semaphore()

    def greet(device):
        pl.semaphore_signal(barrier, inc=1, device_id=device, device_id_type=MESH)

    loop(n_rows, lambda k: greet(in_rows(k)[1]))
    loop(n_group, lambda k: greet(in_group(k)[1]))
    pl.semaphore_wait(barrier, n_rows + n_group - 2)

    send_slabs(hankel, h_slab, 0, pl.ds(0, rows_dev))
    own_copy(hankel, h_slab, 0).wait()
    begin_copy.wait()
    wait_bytes(h_slab.at[pl.ds(0, n_rows - 1)], slab_recv.at[0])
    scatter(product(whole(h_slab), begun[...]), 0)
    send_piece(0)
    block = whole(h_slab)
    gram = product(block, block, NT)
    across(0)
    for piece in range(1, pieces - 1):
        send_piece(piece)
    spread(0)
    y = total(0)
    scatter(product(gram, y), 1)
    y_t = y.T
    back = product(y_t, whole(h_slab))
    across(1)
    send_piece(pieces - 1)
    spread(1)
    c = total(1)
    c_t = c.T

    grams = (product(y_t, c), product(c_t, c) * (1.0 / prefixes))
    blocks = grams[0].shape[0] // 8
    cuts = (blocks // 4, blocks // 2, 3 * blocks // 4)
    grams = eliminate(0, cuts[0], grams)
    own_copy(shifted, s_slab, 1).wait()
    wait_bytes(s_slab.at[pl.ds(0, n_rows - 1)], slab_recv.at[1])
    scatter(product(whole(s_slab), back, NT), 2)
    grams = eliminate(cuts[0], cuts[1], grams)
    across(2)
    grams = eliminate(cuts[1], cuts[2], grams)
    spread(2)
    right_inv, left_inv = eliminate(cuts[2], blocks, grams)
    mine = sums.at[1].reshape(prefixes, c.shape[1])
    basis_out[...] = product(
        mine[pl.ds(pl.multiple_of(row * rows_dev, rows_dev), rows_dev), :], left_inv, NT
    )
    crossed = product(c_t, total(2)) * (1.0 / math.sqrt(prefixes))
    operator_out[...] = product(product(left_inv, crossed), right_inv, NT)

    for which in range(2):
        wait_bytes(h_slab.at[pl.ds(0, n_rows - 1)], slab_send.at[which])
    for which in range(3):
        wait_bytes(parts.at[which, pl.ds(0, n_group - 1)], part_send.at[which])
        wait_bytes(middle.at[which, pl.ds(0, n_layers - 1)], mid_send.at[which])
        wait_bytes(sums.at[which, pl.ds(0, n_group - 1)], sum_send.at[which])


def on_device(hankel, shifted, start_basis):
    n_rows, n_cols = lax.axis_size("rows"), lax.axis_size("cols")
    near = 2
    n_group = near * n_cols
    rows_dev, cols_dev = hankel.shape
    sub, rank = cols_dev // n_rows, start_basis.shape[1]
    share = rows_dev * n_rows // n_group
    slab = pltpu.VMEM((n_rows, rows_dev, sub), jnp.float32)
    grouped = pltpu.VMEM((3, n_group, share, rank), jnp.float32)
    return pl.pallas_call(
        functools.partial(spectral_kernel, n_rows, n_cols, near),
        out_shape=[
            jax.ShapeDtypeStruct((rows_dev, rank), jnp.float32),
            jax.ShapeDtypeStruct((rank, rank), jnp.float32),
        ],
        in_specs=[pl.BlockSpec(memory_space=pltpu.HBM)] * 3,
        out_specs=[pl.BlockSpec(memory_space=pltpu.VMEM)] * 2,
        scratch_shapes=[
            slab,
            slab,
            pltpu.VMEM((sub, rank), jnp.float32),
            grouped,
            grouped,
            pltpu.VMEM((3, n_rows // near, share, rank), jnp.float32),
            grouped,
            pltpu.SemaphoreType.DMA((3,)),
            pltpu.SemaphoreType.DMA((2,)),
            pltpu.SemaphoreType.DMA((2,)),
        ]
        + [pltpu.SemaphoreType.DMA((3,))] * 6,
        compiler_params=pltpu.CompilerParams(
            collective_id=0, has_side_effects=True, vmem_limit_bytes=VMEM_LIMIT
        ),
    )(hankel, shifted, start_basis)


def solution(mesh):
    return jax.shard_map(
        on_device,
        mesh=mesh,
        in_specs=(P("rows", "cols"), P("rows", "cols"), P(("cols", "rows"), None)),
        out_specs=(P("rows", None), P()),
        check_vma=False,
    )
```

time: 743 us -> 85.2 us (0.11)
  waiting for transfers between devices: 602 us -> 0 us
  Pallas kernels: 0 us -> 79.6 us
  other arithmetic: 71.1 us -> 0 us
  matrix products: 30.9 us -> 0 us
  blocking collectives: 21.3 us -> 0 us
  between operations: 14.3 us -> 0.65 us
    psum x3 -> x0, waiting for transfers between devices: 359 us -> none  [the longest x1 122 us: on_device(): lax.psum((product(y_slice.T, y_slice) / total, product(y_slice.T, z_slice...]
    all_gather x2 -> x0, waiting for transfers between devices: 152 us -> none  [the longest x1 78.3 us: on_device(): lax.all_gather(start_basis, 'rows', axis=0, tiled=True)]
    reduce_scatter x1 -> x0, waiting for transfers between devices: 89.3 us -> none  [on_device(): lax.psum_scatter(product(block.T, u_full), 'rows', scatter_dimension=0, t...]
    pallas_call x0 -> x1, Pallas kernels: none -> 79.6 us  [on_device(): pl.pallas_call(functools.partial(spectral_kernel, n_rows, n_cols, near),...]
    another operation x15 -> x0, other arithmetic: 68.6 us -> none  [the longest x6 31.4 us: right_solve(): lax.linalg.triangular_solve(lower, values, left_side=False, lower=True, t...]
    dot_general x8 -> x0, matrix products: 25.3 us -> none  [product(): jnp.dot(left, right, precision=lax.Precision.HIGHEST, preferred_element_t...]
    psum x2 -> x0, blocking collectives: 21.3 us -> none  [the longest x1 11.2 us: on_device(): y_full, z_full = lax.psum((y_part, z_part), 'cols')]
  transfers between devices with their start and end apart: 6 -> 0, of which waited for: 6 -> 0; matrix products, arithmetic and copies ran while one was open for 0% -> 0% of each run, Pallas kernels for 0% -> 0%
where the time goes in v2:
time: 85.2 us; the launch traced here: 85 us
  Pallas kernels  79.6 us (93%)
  local copies, waits for them, and re-layouts  4.72 us (6%)
    pallas_call x1, Pallas kernels, on_device(): pl.pallas_call(functools.partial(spectral_kernel, n_rows, n_cols, near),...  79.6 us
    unnamed x8, local copies, waits for them, and re-layouts  4.72 us

profile of v2, /device:TPU:0, one launch (start us, length us, event | category | flops | bytes accessed | tf_op | source)
XLA Modules:
  0.0 85.0 jit_solution(16240050979213401937)
XLA Ops:
  0.6 0.0 copy-start
  0.6 1.2 %copy-done = f32[32,8192]{1,0:T(8,128)S(1)} copy-done((f32[32,8192]{1,0:T(8,128)S(1)}, f32[32,8192]{1,0:T(8,128)}, u32[]{:S(2)}) %copy-start) | copy-done | bytes 1048600
  1.9 0.0 copy-start.1
  1.9 1.2 %copy-done.1 = f32[32,8192]{1,0:T(8,128)S(1)} copy-done((f32[32,8192]{1,0:T(8,128)S(1)}, f32[32,8192]{1,0:T(8,128)}, u32[]{:S(2)}) %copy-start.1) | copy-done | bytes 1048600
  3.1 0.0 copy-start.2
  3.1 1.0 %copy-done.2 = f32[1024,128]{1,0:T(8,128)S(1)} copy-done((f32[1024,128]{1,0:T(8,128)S(1)}, f32[1024,128]{1,0:T(8,128)}, u32[]{:S(2)}) %copy-start.2) | copy-done | bytes 524312
  4.1 79.6 %shard_map.50 = (f32[32,128]{1,0:T(8,128)S(1)}, f32[128,128]{1,0:T(8,128)S(1)}) custom-call(f32[32,8192]{1,0:T(8,128)S(1)} %copy-done, f32[32,8192]{1,0:T(8,128)S(1)} %copy-done.1, f32[1024,128]{1,0:T(8,128)S(1)} %copy-done.2), custom_call_target="tpu_custom_call" | custom-call | tf_op jit(solution)/shard_map/pallas_call | solution.py:220
  83.7 0.6 copy.7
  84.4 0.6 copy.8
Async XLA Ops:
  0.6 1.2 %copy-start = (f32[32,8192]{1,0:T(8,128)S(1)}, f32[32,8192]{1,0:T(8,128)}, u32[]{:S(2)}) copy-start(f32[32,8192]{1,0:T(8,128)} %hankel.1) | copy-start | bytes 3145732
  1.9 1.2 %copy-start.1 = (f32[32,8192]{1,0:T(8,128)S(1)}, f32[32,8192]{1,0:T(8,128)}, u32[]{:S(2)}) copy-start(f32[32,8192]{1,0:T(8,128)} %shifted.1) | copy-start | bytes 3145732
  3.1 1.0 %copy-start.2 = (f32[1024,128]{1,0:T(8,128)S(1)}, f32[1024,128]{1,0:T(8,128)}, u32[]{:S(2)}) copy-start(f32[1024,128]{1,0:T(8,128)} %start.1) | copy-start | bytes 1572868

commit v3 on v2

--- a/solution.py
+++ b/solution.py
@@ -10,7 +10,7 @@
 
 MESH = pl.DeviceIdType.MESH
 NT = (((1,), (1,)), ((), ()))
-VMEM_LIMIT = 48 * 1024 * 1024
+VMEM_LIMIT = 64 * 1024 * 1024 - 256 * 1024
 
 
 def product(left, right, dims=(((1,), (0,)), ((), ()))):
@@ -26,30 +26,52 @@
 def eliminate(begin, end, grams):
     size = grams[0].shape[0]
     height = 8
-    lane = lax.broadcasted_iota(jnp.int32, (size, size), 1)
-    place = lax.broadcasted_iota(jnp.int32, (size, size), 0)
+    limit = size - height * begin
+    lane = lax.broadcasted_iota(jnp.int32, (limit, size), 1)
+    place = lax.broadcasted_iota(jnp.int32, (limit, size), 0)
     line = lax.broadcasted_iota(jnp.int32, (1, size), 1)
 
     def block(b, held):
-        held = list(held)
+        live = [values[:limit] for values in held]
         pending = size - height * b
-        for r in range(height):
-            active = (place > r) & (place < pending)
+        for r in range(0, height, 2):
+            active = (place > r + 1) & (place < pending)
+            cleared = (lane == r) | (lane == r + 1)
             known = (line < r) | (line >= pending)
-            for m, values in enumerate(held):
-                pivot = values[r : r + 1]
-                diagonal = pivot[:, r : r + 1]
-                inverse = 1.0 / diagonal
-                scaled = jnp.where(line == r, inverse, pivot * inverse)
-                final = jnp.where(known, pivot, jnp.where(line == r, 1.0, 0.0)) * lax.rsqrt(diagonal)
-                kept = jnp.where(lane == r, 0.0, values) - values[:, r : r + 1] * scaled
-                held[m] = jnp.where(active, kept, jnp.where(place == r, final, values))
+            for m, values in enumerate(live):
+                p, q = values[r : r + 1], values[r + 1 : r + 2]
+                d_pp, d_pq, d_qq = p[:, r : r + 1], p[:, r + 1 : r + 2], q[:, r + 1 : r + 2]
+                det = d_pp * d_qq - d_pq * d_pq
+                inverse = 1.0 / det
+                i_pp, i_pq, i_qq = d_qq * inverse, d_pq * inverse, d_pp * inverse
+                first = jnp.where(line == r, i_pp, jnp.where(line == r + 1, -i_pq, p * i_pp - q * i_pq))
+                second = jnp.where(line == r, -i_pq, jnp.where(line == r + 1, i_qq, q * i_qq - p * i_pq))
+                kept = (
+                    jnp.where(cleared, 0.0, values)
+                    - values[:, r : r + 1] * first
+                    - values[:, r + 1 : r + 2] * second
+                )
+                p_known = jnp.where(known, p, jnp.where(line == r, 1.0, 0.0))
+                q_known = jnp.where(known, q, jnp.where(line == r + 1, 1.0, 0.0))
+                upper = p_known * lax.rsqrt(d_pp)
+                under = (q_known - p_known * (d_pq / d_pp)) * lax.rsqrt(det / d_pp)
+                done = jnp.where(place == r, upper, jnp.where(place == r + 1, under, values))
+                live[m] = jnp.where(active, kept, done)
         return tuple(
-            pltpu.roll(jnp.concatenate([values[height:], values[:height]], axis=0), size - height, 1)
-            for values in held
+            pltpu.roll(
+                jnp.concatenate([x for x in (new[height:], values[limit:], new[:height]) if x.size], axis=0),
+                size - height,
+                1,
+            )
+            for new, values in zip(live, held)
         )
 
     return lax.fori_loop(begin, end, block, grams)
+
+
+def unit_scaled(gram):
+    corner = gram[:1, :1]
+    return gram * (1.0 / corner), lax.rsqrt(corner)
 
 
 def spectral_kernel(
@@ -164,26 +186,28 @@
     begin_copy.wait()
     wait_bytes(h_slab.at[pl.ds(0, n_rows - 1)], slab_recv.at[0])
     scatter(product(whole(h_slab), begun[...]), 0)
-    send_piece(0)
     block = whole(h_slab)
     gram = product(block, block, NT)
     across(0)
-    for piece in range(1, pieces - 1):
-        send_piece(piece)
+    send_piece(0)
     spread(0)
     y = total(0)
     scatter(product(gram, y), 1)
     y_t = y.T
     back = product(y_t, whole(h_slab))
     across(1)
-    send_piece(pieces - 1)
+    send_piece(1)
     spread(1)
+    for piece in range(2, pieces):
+        send_piece(piece)
     c = total(1)
     c_t = c.T
 
-    grams = (product(y_t, c), product(c_t, c) * (1.0 / prefixes))
-    blocks = grams[0].shape[0] // 8
-    cuts = (blocks // 4, blocks // 2, 3 * blocks // 4)
+    right_gram, right_scale = unit_scaled(product(y_t, c))
+    left_gram, left_scale = unit_scaled(product(c_t, c) * (1.0 / prefixes))
+    grams = (right_gram, left_gram)
+    blocks = right_gram.shape[0] // 8
+    cuts = (3 * blocks // 8, 5 * blocks // 8, 13 * blocks // 16)
     grams = eliminate(0, cuts[0], grams)
     own_copy(shifted, s_slab, 1).wait()
     wait_bytes(s_slab.at[pl.ds(0, n_rows - 1)], slab_recv.at[1])
@@ -193,6 +217,7 @@
     grams = eliminate(cuts[1], cuts[2], grams)
     spread(2)
     right_inv, left_inv = eliminate(cuts[2], blocks, grams)
+    right_inv, left_inv = right_inv * right_scale, left_inv * left_scale
     mine = sums.at[1].reshape(prefixes, c.shape[1])
     basis_out[...] = product(
         mine[pl.ds(pl.multiple_of(row * rows_dev, rows_dev), rows_dev), :], left_inv, NT

time: 85.2 us -> 87.1 us (1.022)
  Pallas kernels: 79.6 us -> 83.4 us
  local copies, waits for them, and re-layouts: 4.72 us -> 2.8 us
    pallas_call x1, Pallas kernels: 79.6 us -> 83.4 us  [on_device(): pl.pallas_call(functools.partial(spectral_kernel, n_rows, n_cols, near),...]
    unnamed x8 -> x2, local copies, waits for them, and re-layouts: 4.72 us -> 2.8 us
where the time goes in v3:
time: 87.1 us; the launch traced here: 86.9 us
  Pallas kernels  83.4 us (96%)
  local copies, waits for them, and re-layouts  2.8 us (3%)
    pallas_call x1, Pallas kernels, on_device(): pl.pallas_call(functools.partial(spectral_kernel, n_rows, n_cols, near),...  83.4 us
    unnamed x2, local copies, waits for them, and re-layouts  2.8 us

profile of v3, /device:TPU:0, one launch (start us, length us, event | category | flops | bytes accessed | tf_op | source)
XLA Modules:
  0.0 86.9 jit_solution(11508214056423767780)
XLA Ops:
  0.6 83.4 %shard_map.50 = (f32[32,128]{1,0:T(8,128)}, f32[128,128]{1,0:T(8,128)}) custom-call(f32[32,8192]{1,0:T(8,128)} %hankel.1, f32[32,8192]{1,0:T(8,128)} %shifted.1, f32[1024,128]{1,0:T(8,128)} %start.1), custom_call_target="tpu_custom_call" | custom-call | tf_op jit(solution)/shard_map/pallas_call | solution.py:245
  84.1 1.3 %copy.7 = f32[32,128]{1,0:T(8,128)} copy(f32[32,128]{1,0:T(8,128)} %get-tuple-element.4) | data formatting | bytes 32768
  85.4 1.5 %copy.8 = f32[128,128]{1,0:T(8,128)} copy(f32[128,128]{1,0:T(8,128)} %get-tuple-element.5) | data formatting | bytes 131072

commit v4 on v3

--- a/solution.py
+++ b/solution.py
@@ -10,7 +10,7 @@
 
 MESH = pl.DeviceIdType.MESH
 NT = (((1,), (1,)), ((), ()))
-VMEM_LIMIT = 64 * 1024 * 1024 - 256 * 1024
+VMEM_LIMIT = 64 * 1024 * 1024 - 480 * 1024
 
 
 def product(left, right, dims=(((1,), (0,)), ((), ()))):
@@ -185,21 +185,22 @@
     own_copy(hankel, h_slab, 0).wait()
     begin_copy.wait()
     wait_bytes(h_slab.at[pl.ds(0, n_rows - 1)], slab_recv.at[0])
+    send_piece(0)
     scatter(product(whole(h_slab), begun[...]), 0)
     block = whole(h_slab)
     gram = product(block, block, NT)
     across(0)
-    send_piece(0)
+    send_piece(1)
     spread(0)
+    send_piece(2)
     y = total(0)
     scatter(product(gram, y), 1)
     y_t = y.T
     back = product(y_t, whole(h_slab))
     across(1)
-    send_piece(1)
+    for piece in range(3, pieces):
+        send_piece(piece)
     spread(1)
-    for piece in range(2, pieces):
-        send_piece(piece)
     c = total(1)
     c_t = c.T
 
@@ -207,7 +208,7 @@
     left_gram, left_scale = unit_scaled(product(c_t, c) * (1.0 / prefixes))
     grams = (right_gram, left_gram)
     blocks = right_gram.shape[0] // 8
-    cuts = (3 * blocks // 8, 5 * blocks // 8, 13 * blocks // 16)
+    cuts = (blocks // 8, 7 * blocks // 16, 11 * blocks // 16)
     grams = eliminate(0, cuts[0], grams)
     own_copy(shifted, s_slab, 1).wait()
     wait_bytes(s_slab.at[pl.ds(0, n_rows - 1)], slab_recv.at[1])

time: 87.1 us -> 86.7 us (level)
  no operation moved by 1% of the time
where the time goes in v4:
time: 86.7 us; the launch traced here: 86.5 us
  Pallas kernels  83 us (96%)
  local copies, waits for them, and re-layouts  2.8 us (3%)
    pallas_call x1, Pallas kernels, on_device(): pl.pallas_call(functools.partial(spectral_kernel, n_rows, n_cols, near),...  83 us
    unnamed x2, local copies, waits for them, and re-layouts  2.8 us

profile of v4, /device:TPU:0, one launch (start us, length us, event | category | flops | bytes accessed | tf_op | source)
XLA Modules:
  0.0 86.5 jit_solution(3694121350317658464)
XLA Ops:
  0.6 83.0 %shard_map.50 = (f32[32,128]{1,0:T(8,128)}, f32[128,128]{1,0:T(8,128)}) custom-call(f32[32,8192]{1,0:T(8,128)} %hankel.1, f32[32,8192]{1,0:T(8,128)} %shifted.1, f32[1024,128]{1,0:T(8,128)} %start.1), custom_call_target="tpu_custom_call" | custom-call | tf_op jit(solution)/shard_map/pallas_call | solution.py:246
  83.7 1.3 %copy.7 = f32[32,128]{1,0:T(8,128)} copy(f32[32,128]{1,0:T(8,128)} %get-tuple-element.4) | data formatting | bytes 32768
  85.0 1.5 %copy.8 = f32[128,128]{1,0:T(8,128)} copy(f32[128,128]{1,0:T(8,128)} %get-tuple-element.5) | data formatting | bytes 131072

commit v5 on v2

--- a/solution.py
+++ b/solution.py
@@ -10,7 +10,7 @@
 
 MESH = pl.DeviceIdType.MESH
 NT = (((1,), (1,)), ((), ()))
-VMEM_LIMIT = 48 * 1024 * 1024
+VMEM_LIMIT = 64 * 1024 * 1024 - 480 * 1024
 
 
 def product(left, right, dims=(((1,), (0,)), ((), ()))):
@@ -24,37 +24,50 @@
 
 
 def eliminate(begin, end, grams):
-    size = grams[0].shape[0]
-    height = 8
-    lane = lax.broadcasted_iota(jnp.int32, (size, size), 1)
-    place = lax.broadcasted_iota(jnp.int32, (size, size), 0)
+    height, size = grams[0][0].shape
+    tiles = len(grams[0])
+    lane = lax.broadcasted_iota(jnp.int32, (height, size), 1)
+    sublane = lax.broadcasted_iota(jnp.int32, (height, size), 0)
     line = lax.broadcasted_iota(jnp.int32, (1, size), 1)
 
     def block(b, held):
-        held = list(held)
-        pending = size - height * b
+        held = [list(matrix) for matrix in held]
+        known_from = size - height * b
         for r in range(height):
-            active = (place > r) & (place < pending)
-            known = (line < r) | (line >= pending)
-            for m, values in enumerate(held):
-                pivot = values[r : r + 1]
+            here = lane == r
+            known = (line < r) | (line >= known_from)
+            for matrix in held:
+                pivot = matrix[0][r : r + 1]
                 diagonal = pivot[:, r : r + 1]
                 inverse = 1.0 / diagonal
-                scaled = jnp.where(line == r, inverse, pivot * inverse)
+                scaled = jnp.broadcast_to(jnp.where(line == r, inverse, pivot * inverse), (height, size))
                 final = jnp.where(known, pivot, jnp.where(line == r, 1.0, 0.0)) * lax.rsqrt(diagonal)
-                kept = jnp.where(lane == r, 0.0, values) - values[:, r : r + 1] * scaled
-                held[m] = jnp.where(active, kept, jnp.where(place == r, final, values))
+                for i in range(tiles - begin):
+                    values = matrix[i]
+                    kept = jnp.where(here, 0.0, values) - values[:, r : r + 1] * scaled
+                    if i == 0:
+                        kept = jnp.where(sublane > r, kept, jnp.where(sublane == r, final, values))
+                    elif i > tiles - end:
+                        kept = jnp.where(i < tiles - b, kept, values)
+                    matrix[i] = kept
         return tuple(
-            pltpu.roll(jnp.concatenate([values[height:], values[:height]], axis=0), size - height, 1)
-            for values in held
+            tuple(pltpu.roll(values, size - height, 1) for values in matrix[1:] + matrix[:1]) for matrix in held
         )
 
     return lax.fori_loop(begin, end, block, grams)
+
+
+def to_tiles(gram):
+    return tuple(gram[i : i + 8] for i in range(0, gram.shape[0], 8))
+
+
+def from_tiles(tiles):
+    return jnp.concatenate(tiles, axis=0)
 
 
 def spectral_kernel(
     n_rows, n_cols, near, hankel, shifted, start, basis_out, operator_out,
-    h_slab, s_slab, begun, parts, landed, middle, sums, local_sem, slab_send, slab_recv,
+    h_own, s_own, h_slab, s_slab, begun, parts, landed, middle, sums, local_sem, slab_send, slab_recv,
     part_send, part_recv, mid_send, mid_recv, sum_send, sum_recv,
 ):
     row, col = lax.axis_index("rows"), lax.axis_index("cols")
@@ -101,6 +114,9 @@
     def own_copy(source, slab, which):
         return pltpu.make_async_copy(source.at[:, own_columns(row)], slab.at[row], local_sem.at[which])
 
+    hankel_in = pltpu.make_async_copy(hankel, h_own, local_sem.at[3])
+    shifted_in = pltpu.make_async_copy(shifted, s_own, local_sem.at[4])
+
     def send_slabs(source, slab, which, lines):
         def body(k):
             other, device = in_rows(k)
@@ -115,7 +131,7 @@
         loop(n_rows, body)
 
     def send_piece(piece):
-        send_slabs(shifted, s_slab, 1, pl.ds(8 * piece, 8))
+        send_slabs(s_own, s_slab, 1, pl.ds(8 * piece, 8))
 
     def whole(slab):
         return slab[...].reshape(prefixes, sub)
@@ -146,7 +162,9 @@
         wait_bytes(sums.at[which, pl.ds(0, n_group - 1)], sum_recv.at[which])
         return sums[which].reshape(prefixes, sums.shape[3])
 
+    hankel_in.start()
     own_copy(hankel, h_slab, 0).start()
+    shifted_in.start()
     own_copy(shifted, s_slab, 1).start()
     begin_copy = pltpu.make_async_copy(start, begun, local_sem.at[2])
     begin_copy.start()
@@ -159,31 +177,34 @@
     loop(n_group, lambda k: greet(in_group(k)[1]))
     pl.semaphore_wait(barrier, n_rows + n_group - 2)
 
-    send_slabs(hankel, h_slab, 0, pl.ds(0, rows_dev))
+    hankel_in.wait()
+    send_slabs(h_own, h_slab, 0, pl.ds(0, rows_dev))
+    shifted_in.wait()
     own_copy(hankel, h_slab, 0).wait()
     begin_copy.wait()
     wait_bytes(h_slab.at[pl.ds(0, n_rows - 1)], slab_recv.at[0])
+    send_piece(0)
     scatter(product(whole(h_slab), begun[...]), 0)
-    send_piece(0)
     block = whole(h_slab)
     gram = product(block, block, NT)
     across(0)
-    for piece in range(1, pieces - 1):
-        send_piece(piece)
+    send_piece(1)
     spread(0)
+    send_piece(2)
     y = total(0)
     scatter(product(gram, y), 1)
     y_t = y.T
     back = product(y_t, whole(h_slab))
     across(1)
-    send_piece(pieces - 1)
+    for piece in range(3, pieces):
+        send_piece(piece)
     spread(1)
     c = total(1)
     c_t = c.T
 
-    grams = (product(y_t, c), product(c_t, c) * (1.0 / prefixes))
-    blocks = grams[0].shape[0] // 8
-    cuts = (blocks // 4, blocks // 2, 3 * blocks // 4)
+    grams = (to_tiles(product(y_t, c)), to_tiles(product(c_t, c) * (1.0 / prefixes)))
+    blocks = len(grams[0])
+    cuts = (blocks // 8, 7 * blocks // 16, 11 * blocks // 16)
     grams = eliminate(0, cuts[0], grams)
     own_copy(shifted, s_slab, 1).wait()
     wait_bytes(s_slab.at[pl.ds(0, n_rows - 1)], slab_recv.at[1])
@@ -193,6 +214,7 @@
     grams = eliminate(cuts[1], cuts[2], grams)
     spread(2)
     right_inv, left_inv = eliminate(cuts[2], blocks, grams)
+    right_inv, left_inv = from_tiles(right_inv), from_tiles(left_inv)
     mine = sums.at[1].reshape(prefixes, c.shape[1])
     basis_out[...] = product(
         mine[pl.ds(pl.multiple_of(row * rows_dev, rows_dev), rows_dev), :], left_inv, NT
@@ -226,6 +248,8 @@
         in_specs=[pl.BlockSpec(memory_space=pltpu.HBM)] * 3,
         out_specs=[pl.BlockSpec(memory_space=pltpu.VMEM)] * 2,
         scratch_shapes=[
+            pltpu.VMEM((rows_dev, cols_dev), jnp.float32),
+            pltpu.VMEM((rows_dev, cols_dev), jnp.float32),
             slab,
             slab,
             pltpu.VMEM((sub, rank), jnp.float32),
@@ -233,7 +257,7 @@
             grouped,
             pltpu.VMEM((3, n_rows // near, share, rank), jnp.float32),
             grouped,
-            pltpu.SemaphoreType.DMA((3,)),
+            pltpu.SemaphoreType.DMA((5,)),
             pltpu.SemaphoreType.DMA((2,)),
             pltpu.SemaphoreType.DMA((2,)),
         ]

time: 85.2 us -> 81.7 us (0.959)
  local copies, waits for them, and re-layouts: 4.72 us -> 2.8 us
  Pallas kernels: 79.6 us -> 78.1 us
    unnamed x8 -> x2, local copies, waits for them, and re-layouts: 4.72 us -> 2.8 us
    pallas_call x1, Pallas kernels: 79.6 us -> 78.1 us  [on_device(): pl.pallas_call(functools.partial(spectral_kernel, n_rows, n_cols, near),...]
where the time goes in v5:
time: 81.7 us; the launch traced here: 81.5 us
  Pallas kernels  78.1 us (96%)
  local copies, waits for them, and re-layouts  2.8 us (3%)
    pallas_call x1, Pallas kernels, on_device(): pl.pallas_call(functools.partial(spectral_kernel, n_rows, n_cols, near),...  78.1 us
    unnamed x2, local copies, waits for them, and re-layouts  2.8 us

profile of v5, /device:TPU:0, one launch (start us, length us, event | category | flops | bytes accessed | tf_op | source)
XLA Modules:
  0.0 81.5 jit_solution(11640348798694563518)
XLA Ops:
  0.6 78.1 %shard_map.50 = (f32[32,128]{1,0:T(8,128)}, f32[128,128]{1,0:T(8,128)}) custom-call(f32[32,8192]{1,0:T(8,128)} %hankel.1, f32[32,8192]{1,0:T(8,128)} %shifted.1, f32[1024,128]{1,0:T(8,128)} %start.1), custom_call_target="tpu_custom_call" | custom-call | tf_op jit(solution)/shard_map/pallas_call | solution.py:242
  78.7 1.3 %copy.7 = f32[32,128]{1,0:T(8,128)} copy(f32[32,128]{1,0:T(8,128)} %get-tuple-element.4) | data formatting | bytes 32768
  80.0 1.5 %copy.8 = f32[128,128]{1,0:T(8,128)} copy(f32[128,128]{1,0:T(8,128)} %get-tuple-element.5) | data formatting | bytes 131072

commit v6 on v5

--- a/solution.py
+++ b/solution.py
@@ -17,6 +17,18 @@
     return lax.dot_general(
         left, right, dims, precision=lax.Precision.HIGHEST, preferred_element_type=jnp.float32
     )
+
+
+def split(values):
+    high = values.astype(jnp.bfloat16)
+    return high, (values - high.astype(jnp.float32)).astype(jnp.bfloat16)
+
+
+def split_product(left, right, dims=(((1,), (0,)), ((), ()))):
+    def term(a, b):
+        return lax.dot_general(a, b, dims, preferred_element_type=jnp.float32)
+
+    return term(left[0], right[0]) + (term(left[0], right[1]) + term(left[1], right[0]))
 
 
 def wait_bytes(ref, sem):
@@ -184,19 +196,18 @@
     begin_copy.wait()
     wait_bytes(h_slab.at[pl.ds(0, n_rows - 1)], slab_recv.at[0])
     send_piece(0)
-    scatter(product(whole(h_slab), begun[...]), 0)
-    block = whole(h_slab)
-    gram = product(block, block, NT)
+    block = split(whole(h_slab))
+    scatter(split_product(block, split(begun[...])), 0)
+    gram = split_product(block, block, NT)
     across(0)
     send_piece(1)
     spread(0)
-    send_piece(2)
     y = total(0)
     scatter(product(gram, y), 1)
     y_t = y.T
-    back = product(y_t, whole(h_slab))
+    back = split(split_product(split(y_t), block))
     across(1)
-    for piece in range(3, pieces):
+    for piece in range(2, pieces):
         send_piece(piece)
     spread(1)
     c = total(1)
@@ -204,11 +215,11 @@
 
     grams = (to_tiles(product(y_t, c)), to_tiles(product(c_t, c) * (1.0 / prefixes)))
     blocks = len(grams[0])
-    cuts = (blocks // 8, 7 * blocks // 16, 11 * blocks // 16)
+    cuts = (5 * blocks // 16, 9 * blocks // 16, 3 * blocks // 4)
     grams = eliminate(0, cuts[0], grams)
     own_copy(shifted, s_slab, 1).wait()
     wait_bytes(s_slab.at[pl.ds(0, n_rows - 1)], slab_recv.at[1])
-    scatter(product(whole(s_slab), back, NT), 2)
+    scatter(split_product(split(whole(s_slab)), back, NT), 2)
     grams = eliminate(cuts[0], cuts[1], grams)
     across(2)
     grams = eliminate(cuts[1], cuts[2], grams)

time: 81.7 us -> 86.3 us (1.056)
  Pallas kernels: 78.1 us -> 82.7 us
    pallas_call x1, Pallas kernels: 78.1 us -> 82.7 us  [on_device(): pl.pallas_call(functools.partial(spectral_kernel, n_rows, n_cols, near),...]
where the time goes in v6:
time: 86.3 us; the launch traced here: 86.1 us
  Pallas kernels  82.7 us (96%)
  local copies, waits for them, and re-layouts  2.8 us (3%)
    pallas_call x1, Pallas kernels, on_device(): pl.pallas_call(functools.partial(spectral_kernel, n_rows, n_cols, near),...  82.7 us
    unnamed x2, local copies, waits for them, and re-layouts  2.8 us

profile of v6, /device:TPU:0, one launch (start us, length us, event | category | flops | bytes accessed | tf_op | source)
XLA Modules:
  0.0 86.1 jit_solution(529720553520052384)
XLA Ops:
  0.6 82.7 %shard_map.50 = (f32[32,128]{1,0:T(8,128)}, f32[128,128]{1,0:T(8,128)}) custom-call(f32[32,8192]{1,0:T(8,128)} %hankel.1, f32[32,8192]{1,0:T(8,128)} %shifted.1, f32[1024,128]{1,0:T(8,128)} %start.1), custom_call_target="tpu_custom_call" | custom-call | tf_op jit(solution)/shard_map/pallas_call | solution.py:253
  83.3 1.3 %copy.7 = f32[32,128]{1,0:T(8,128)} copy(f32[32,128]{1,0:T(8,128)} %get-tuple-element.4) | data formatting | bytes 32768
  84.6 1.5 %copy.8 = f32[128,128]{1,0:T(8,128)} copy(f32[128,128]{1,0:T(8,128)} %get-tuple-element.5) | data formatting | bytes 131072

commit v7 on v6

--- a/solution.py
+++ b/solution.py
@@ -194,20 +194,22 @@
     shifted_in.wait()
     own_copy(hankel, h_slab, 0).wait()
     begin_copy.wait()
+    wait_bytes(h_slab.at[pl.ds(0, n_rows - 1)], slab_send.at[0])
+    send_piece(0)
     wait_bytes(h_slab.at[pl.ds(0, n_rows - 1)], slab_recv.at[0])
-    send_piece(0)
     block = split(whole(h_slab))
     scatter(split_product(block, split(begun[...])), 0)
     gram = split_product(block, block, NT)
     across(0)
     send_piece(1)
     spread(0)
+    send_piece(2)
     y = total(0)
     scatter(product(gram, y), 1)
     y_t = y.T
     back = split(split_product(split(y_t), block))
     across(1)
-    for piece in range(2, pieces):
+    for piece in range(3, pieces):
         send_piece(piece)
     spread(1)
     c = total(1)
@@ -215,7 +217,7 @@
 
     grams = (to_tiles(product(y_t, c)), to_tiles(product(c_t, c) * (1.0 / prefixes)))
     blocks = len(grams[0])
-    cuts = (5 * blocks // 16, 9 * blocks // 16, 3 * blocks // 4)
+    cuts = (blocks // 8, 7 * blocks // 16, 11 * blocks // 16)
     grams = eliminate(0, cuts[0], grams)
     own_copy(shifted, s_slab, 1).wait()
     wait_bytes(s_slab.at[pl.ds(0, n_rows - 1)], slab_recv.at[1])
@@ -233,8 +235,7 @@
     crossed = product(c_t, total(2)) * (1.0 / math.sqrt(prefixes))
     operator_out[...] = product(product(left_inv, crossed), right_inv, NT)
 
-    for which in range(2):
-        wait_bytes(h_slab.at[pl.ds(0, n_rows - 1)], slab_send.at[which])
+    wait_bytes(s_slab.at[pl.ds(0, n_rows - 1)], slab_send.at[1])
     for which in range(3):
         wait_bytes(parts.at[which, pl.ds(0, n_group - 1)], part_send.at[which])
         wait_bytes(middle.at[which, pl.ds(0, n_layers - 1)], mid_send.at[which])

time: 86.3 us -> 82 us (0.950)
  Pallas kernels: 82.7 us -> 78.3 us
    pallas_call x1, Pallas kernels: 82.7 us -> 78.3 us  [on_device(): pl.pallas_call(functools.partial(spectral_kernel, n_rows, n_cols, near),...]
where the time goes in v7:
time: 82 us; the launch traced here: 81.8 us
  Pallas kernels  78.3 us (95%)
  local copies, waits for them, and re-layouts  2.8 us (3%)
    pallas_call x1, Pallas kernels, on_device(): pl.pallas_call(functools.partial(spectral_kernel, n_rows, n_cols, near),...  78.3 us
    unnamed x2, local copies, waits for them, and re-layouts  2.8 us

profile of v7, /device:TPU:0, one launch (start us, length us, event | category | flops | bytes accessed | tf_op | source)
XLA Modules:
  0.0 81.8 jit_solution(9568054642089883573)
XLA Ops:
  0.6 78.3 %shard_map.50 = (f32[32,128]{1,0:T(8,128)}, f32[128,128]{1,0:T(8,128)}) custom-call(f32[32,8192]{1,0:T(8,128)} %hankel.1, f32[32,8192]{1,0:T(8,128)} %shifted.1, f32[1024,128]{1,0:T(8,128)} %start.1), custom_call_target="tpu_custom_call" | custom-call | tf_op jit(solution)/shard_map/pallas_call | solution.py:254
  79.0 1.3 %copy.7 = f32[32,128]{1,0:T(8,128)} copy(f32[32,128]{1,0:T(8,128)} %get-tuple-element.4) | data formatting | bytes 32768
  80.3 1.5 %copy.8 = f32[128,128]{1,0:T(8,128)} copy(f32[128,128]{1,0:T(8,128)} %get-tuple-element.5) | data formatting | bytes 131072

commit v8 on v7

--- a/solution.py
+++ b/solution.py
@@ -199,18 +199,18 @@
     wait_bytes(h_slab.at[pl.ds(0, n_rows - 1)], slab_recv.at[0])
     block = split(whole(h_slab))
     scatter(split_product(block, split(begun[...])), 0)
+    send_piece(1)
     gram = split_product(block, block, NT)
     across(0)
-    send_piece(1)
+    send_piece(2)
     spread(0)
-    send_piece(2)
+    for piece in range(3, pieces):
+        send_piece(piece)
     y = total(0)
     scatter(product(gram, y), 1)
     y_t = y.T
     back = split(split_product(split(y_t), block))
     across(1)
-    for piece in range(3, pieces):
-        send_piece(piece)
     spread(1)
     c = total(1)
     c_t = c.T

time: 82 us -> 85.5 us (1.043)
  Pallas kernels: 78.3 us -> 81.8 us
    pallas_call x1, Pallas kernels: 78.3 us -> 81.8 us  [on_device(): pl.pallas_call(functools.partial(spectral_kernel, n_rows, n_cols, near),...]
where the time goes in v8:
time: 85.5 us; the launch traced here: 85.2 us
  Pallas kernels  81.8 us (96%)
  local copies, waits for them, and re-layouts  2.8 us (3%)
    pallas_call x1, Pallas kernels, on_device(): pl.pallas_call(functools.partial(spectral_kernel, n_rows, n_cols, near),...  81.8 us
    unnamed x2, local copies, waits for them, and re-layouts  2.8 us

profile of v8, /device:TPU:0, one launch (start us, length us, event | category | flops | bytes accessed | tf_op | source)
XLA Modules:
  0.0 85.2 jit_solution(6486833777856479553)
XLA Ops:
  0.6 81.8 %shard_map.50 = (f32[32,128]{1,0:T(8,128)}, f32[128,128]{1,0:T(8,128)}) custom-call(f32[32,8192]{1,0:T(8,128)} %hankel.1, f32[32,8192]{1,0:T(8,128)} %shifted.1, f32[1024,128]{1,0:T(8,128)} %start.1), custom_call_target="tpu_custom_call" | custom-call | tf_op jit(solution)/shard_map/pallas_call | solution.py:254
  82.4 1.3 %copy.7 = f32[32,128]{1,0:T(8,128)} copy(f32[32,128]{1,0:T(8,128)} %get-tuple-element.4) | data formatting | bytes 32768
  83.8 1.5 %copy.8 = f32[128,128]{1,0:T(8,128)} copy(f32[128,128]{1,0:T(8,128)} %get-tuple-element.5) | data formatting | bytes 131072
